TPU v7x, 128 devices: a whole 4x4x4 slice. The times are simulated.
128 devices in a mesh: row: 16 (over z_lo, y, core), cand: 8 (over z_hi, x).
Axes of the slice: x: 4, y: 4, z: 4 (z_hi: 2, z_lo: 2; z = z_hi * 2 + z_lo), core: 2. Of those that a mesh axis runs over, the one named last changes fastest.
Arguments:
- embeddings: bfloat16 [131072, 768], P('row')
- pick_index: int32 [64], replicated, may hold values from 0 to 131071
- cand_index: int32 [8192], replicated, may hold values from 0 to 131071
Outputs:
- gains: float32 [8192], P('cand')
- coverage: float32 [131072], P('row')
All inputs are finite; a program needn't handle non-finite values.
Results may differ from a plain program's by a relative error of at most 0.0003.
Values may be sent and summed in bfloat16 or wider, within the bound.
A program may use at most 128 MiB of HBM per device.

v0:
```python
import jax
import jax.numpy as jnp
from jax import lax
from jax.sharding import PartitionSpec as P


def select_owned(embeddings, indices):
    count = embeddings.shape[0]
    local = indices - lax.axis_index("row") * count
    owned = (local >= 0) & (local < count)
    taken = jnp.take(embeddings, jnp.clip(local, 0, count - 1), axis=0)
    return jnp.where(owned[:, None], taken, jnp.zeros_like(taken))


def inner(left, right):
    return lax.dot_general(
        left, right, (((1,), (1,)), ((), ())), preferred_element_type=jnp.float32
    )


def per_device(embeddings, pick_index, cand_index):
    count = embeddings.shape[0]
    picked = (
        lax.psum(select_owned(embeddings, pick_index), "row")
        .astype(jnp.float32)
        .astype(jnp.bfloat16)
    )
    coverage = jnp.max(inner(embeddings, picked), axis=1)
    per_column = cand_index.shape[0] // lax.axis_size("cand")
    every = (
        lax.psum(select_owned(embeddings, cand_index), "row")
        .astype(jnp.float32)
        .astype(jnp.bfloat16)
    )
    chosen = lax.dynamic_slice_in_dim(every, lax.axis_index("cand") * per_column, per_column, 0)
    similar = inner(embeddings, chosen)
    partial_gain = jnp.sum(jnp.maximum(similar - coverage[:, None], 0.0), axis=0)
    total_rows = count * lax.axis_size("row")
    gains = lax.psum(partial_gain, "row") / total_rows
    return (gains, coverage)


def solution(mesh):
    return jax.shard_map(
        per_device,
        mesh=mesh,
        in_specs=(P("row", None), P(), P()),
        out_specs=(P("cand"), P("row")),
        check_vma=False,
    )
```

profile of v0, /device:TPU:1, one launch (start us, length us, event | category | flops | bytes accessed | tf_op | source)
XLA Modules:
  0.0 297.2 jit_solution(3463207593277725131)
XLA Ops:
  7.2 0.0 all-reduce.3.cloned.1.call-start
  7.2 0.8 compare_and_fusion.1
  8.0 0.8 fusion.1
  8.8 0.7 compare_and_fusion.2
  9.5 7.0 %gather_fusion.1 = bf16[64,768]{1,0:T(8,128)(2,1)S(1)} fusion(bf16[8192,768]{1,0:T(8,128)(2,1)} %param.3, s32[1024]{0:T(1024)S(1)} %pad_clamp_fusion), kind=kCustom, calls=%fused_computation.1 | custom fusion | bytes 196864 | tf_op jit(solution)/shard_map/jit(_take)/gather | solution.py:11
  16.4 43.3 %gather_fusion = bf16[8192,768]{1,0:T(8,128)(2,1)} fusion(bf16[8192,768]{1,0:T(8,128)(2,1)} %param.3, s32[8192]{0:T(1024)S(1)} %fusion.1), kind=kCustom, calls=%fused_computation | custom fusion | bytes 25198592 | tf_op jit(solution)/shard_map/jit(_take)/gather | solution.py:11
  59.7 0.7 select_select_fusion.1
  60.4 13.0 %select_select_fusion = bf16[8192,768]{1,0:T(8,128)(2,1)} fusion(bf16[8192,768]{1,0:T(8,128)(2,1)} %gather_fusion, pred[8192]{0:T(1024)(128)(4,1)S(1)} %get-tuple-element.7, pred[8192]{0:T(1024)(128)(4,1)S(1)} %get-tuple-element.6), kind=kLoop, calls=%fused_computation.3 | loop fusion | flops 12582912 | bytes 25182208 | tf_op jit(solution)/shard_map/jit(_where)/select_n | solution.py:12
  73.5 0.0 all-reduce.3.cloned.1.call-update
  73.5 162.3 %all-reduce.3.cloned.1.call-done = (bf16[64,768]{1,0:T(8,128)(2,1)}, bf16[8192,768]{1,0:T(8,128)(2,1)}) async-done(((bf16[64,768]{1,0:T(8,128)(2,1)}, bf16[8192,768]{1,0:T(8,128)(2,1)}), (bf16[64,768]{1,0:T(8,128)(2,1)}, bf16[8192,768]{1,0:T(8,128)(2,1)})) %all-reduce.3.cloned.1.call-update) | async-done | bytes 12681232 | tf_op jit(solution)/shard_map/psum | solution.py:24
  235.8 8.5 %convolution_reduce_fusion = f32[8192]{0:T(1024)S(1)} fusion(bf16[64,768]{1,0:T(8,128)(2,1)} %get-tuple-element.2, bf16[8192,768]{1,0:T(8,128)(2,1)} %param.3), kind=kOutput, calls=%fused_computation.5 | convolution fusion | flops 805822464 | bytes 12713984 | tf_op jit(solution)/shard_map/dot_general | solution.py:16
  244.3 0.0 copy-start
  244.3 16.8 %maximum_reduce_fusion = f32[1024]{0:T(1024)S(1)} fusion(bf16[8192,768]{1,0:T(8,128)(2,1)} %param.3, f32[8192]{0:T(1024)S(1)} %convolution_reduce_fusion, bf16[8192,768]{1,0:T(8,128)(2,1)} %get-tuple-element.3, s32[]{:T(128)S(6)} %select_n.32), kind=kOutput, calls=%fused_computation.2 | convolution fusion | flops 12910066688 | bytes 14192644 | tf_op jit(solution)/shard_map/dot_general | solution.py:16
  261.1 0.0 copy-done
  261.1 28.6 %psum.23 = f32[1024]{0:T(1024)S(1)} all-reduce(f32[1024]{0:T(1024)S(1)} %maximum_reduce_fusion), channel_id=1, replica_groups=mesh['row'=16,'cand'=8] {'row'}, use_global_device_ids=true, to_apply=%region_4.5 | all-reduce | flops 1024 | bytes 8192 | tf_op jit(solution)/shard_map/psum | solution.py:39
  289.7 0.6 broadcast_multiply_fusion
  (1 shorter events, 0.0 us)
Async XLA Ops:
  7.2 228.6 %all-reduce.3.cloned.1.call-start = ((), (), s32[]{:S(2)}) async-start(), calls=%async_computation | async-start | bytes 25362432 | tf_op jit(solution)/shard_map/psum | solution.py:24
  244.3 16.8 %copy-start = (f32[8192]{0:T(1024)}, f32[8192]{0:T(1024)S(1)}, u32[]{:S(2)}) copy-start(f32[8192]{0:T(1024)S(1)} %convolution_reduce_fusion) | copy-start | bytes 98308
Sparse Core Ops, SparseCore 0:
  73.6 162.1 all-reduce.2
where the time goes:
time: 299 us; the launch traced here: 297 us
  waiting for transfers between devices  162 us (54%)
  local copies, waits for them, and re-layouts  50.2 us (17%)
  blocking collectives  28.6 us (10%)
  matrix products  25.3 us (8%)
  other arithmetic  16.6 us (6%)
  between operations  14.1 us (5%)
    psum x1, waiting for transfers between devices, per_device(): lax.psum(select_owned(embeddings, pick_index), 'row').astype(jnp.float32)  162 us
    gather x2, local copies, waits for them, and re-layouts, select_owned(): taken = jnp.take(embeddings, jnp.clip(local, 0, count - 1), axis=0)  50.2 us
    psum x1, blocking collectives, per_device(): gains = lax.psum(partial_gain, 'row') / total_rows  28.6 us
    dot_general x2, matrix products, inner(): lax.dot_general(left, right, (((1,), (1,)), ((), ())), preferred_element_...  25.3 us
    select_n x2, other arithmetic, select_owned(): return jnp.where(owned[:, None], taken, jnp.zeros_like(taken))  13.8 us
  transfers between devices with their start and end apart: 1, of which 1 were waited for; matrix products, arithmetic and copies ran while one was open for 0% of the time, Pallas kernels for 0%

commit v1 on v0

v1 whole, which is shorter than its diff:
```python
import functools

import jax
import jax.numpy as jnp
from jax import lax
from jax.experimental import pallas as pl
from jax.experimental.pallas import tpu as pltpu
from jax.sharding import PartitionSpec as P

MESH = pl.DeviceIdType.MESH
F32 = jnp.float32
BF16 = jnp.bfloat16

CHIPS = ((0, 0), (1, 0), (0, 1), (0, 3), (1, 1), (1, 3), (0, 2), (1, 2))
ORDER = tuple((dz, dy, dc) for dz, dy in CHIPS for dc in (0, 1))
SLOT = {rel: j for j, rel in enumerate(ORDER)}
OWNERS = 16
CAP = 96
PCAP = 16
TILES = ((0, 192, 0, 4), (192, 432, 2, 8), (432, 704, 5, 12), (704, 1024, 9, 16))
PER = 1024
PICKS = 64


def iota(shape, dim):
    return lax.broadcasted_iota(jnp.int32, shape, dim)


def dot(a, b):
    return jnp.dot(a, b, preferred_element_type=F32)


def inner(left, right):
    return lax.dot_general(left, right, (((1,), (1,)), ((), ())), preferred_element_type=F32)


def ones_where(cond):
    return jnp.where(cond, 1.0, 0.0).astype(BF16)


def order_of(owner, device):
    dz = (owner >> 3) ^ (device >> 3)
    dy = ((owner >> 1) - (device >> 1)) & 3
    chip = dz * 4 + dy
    place = jnp.zeros_like(chip)
    for rank, (cz, cy) in enumerate(CHIPS):
        place = jnp.where(chip == cz * 4 + cy, rank, place)
    return place * 2 + ((owner ^ device) & 1)


def kernel(
    block_rows, shift,
    cand_ref, pick_ref, pick_col_ref, emb_hbm,
    gains_ref, cover_ref, flag_ref,
    emb, blk, pk, ch, acc, red,
    load_sem, pk_send, pk_recv, blk_send, blk_recv, red_send, red_recv,
):
    rows = emb.shape[0]
    chunks = load_sem.shape[0]
    chunk = rows // chunks
    me = lax.axis_index("row")
    group = lax.axis_index("cand")
    z, y, c = me // 8, (me // 2) % 4, me % 2

    def device(dz, dy, dc):
        return (z + dz) % 2 * 8 + (y + dy) % 4 * 2 + (c + dc) % 2

    def load(i):
        at = pl.ds(pl.multiple_of(i * chunk, chunk), chunk)
        return pltpu.make_async_copy(emb_hbm.at[at], emb.at[at], load_sem.at[i])

    for i in range(chunks):
        load(i).start()

    barrier = pltpu.get_barrier_semaphore()
    for rel in ORDER[1:]:
        pl.semaphore_signal(barrier, inc=1, device_id={"row": device(*rel)}, device_id_type=MESH)

    mine = cand_ref[pl.ds(pl.multiple_of(group * 8, 8), 8), :]
    owner, local = mine >> shift, mine & (rows - 1)
    masks = [owner == device(*rel) for rel in ORDER]
    mask = jnp.concatenate([jnp.where(m, 1.0, 0.0) for m in masks], axis=0).astype(BF16)
    r0, r1 = iota((128, 128), 0), iota((128, 128), 1)
    before = ones_where(r0 < r1)
    within = dot(mask, before)
    totals = dot(mask, jnp.ones((128, 128), BF16)).astype(BF16)
    same = (r0 >> 3) == (r1 >> 3)
    rank = within + dot(ones_where(same & (r1 < r0)), totals)
    count = dot(ones_where(same), totals)
    base = dot(ones_where((r1 >> 3) < (r0 >> 3)), totals)
    place = jnp.zeros((8, 128), F32)
    for j in range(OWNERS):
        at = slice(8 * j, 8 * j + 8)
        place += jnp.where(masks[j], rank[at] + base[at], 0.0)

    key = jnp.where(masks[0], rank[:8], -1.0)
    local_plus = (local + 1).astype(F32)
    slot_row = jnp.zeros((CAP, 128), F32)
    slots = iota((CAP, 128), 0).astype(F32)
    for r in range(8):
        slot_row += jnp.where(slots == key[r:r + 1], local_plus[r:r + 1], 0.0)
    cand_at = jnp.sum(slot_row, axis=1, keepdims=True)
    pick = pick_ref[...]
    pick_mine = jnp.broadcast_to((pick >> shift) == me, (8, 128))
    pick_rank = dot(ones_where(pick_mine), before)
    pick_key = jnp.where(pick_mine, pick_rank, -1.0)
    pick_plus = ((pick & (rows - 1)) + 1).astype(F32)
    pick_at = jnp.sum(
        jnp.where(iota((PCAP, 128), 0).astype(F32) == pick_key[:1], pick_plus, 0.0),
        axis=1, keepdims=True)
    at_row = jnp.concatenate([cand_at, pick_at], axis=0).astype(jnp.int32) - 1
    at_row = jnp.broadcast_to(at_row, (CAP + PCAP, chunk))

    lanes = iota((CAP + PCAP, chunk), 1)

    def gather(i, total):
        load(i).wait()
        at = pl.ds(pl.multiple_of(i * chunk, chunk), chunk)
        return total + dot(ones_where(at_row - i * chunk == lanes), emb[at, :])

    total = lax.fori_loop(0, chunks, gather, jnp.zeros((CAP + PCAP, emb.shape[1]), F32))
    pk[0] = total[CAP:].astype(BF16)
    blk[0] = total[:CAP].astype(BF16)

    pl.semaphore_wait(barrier, OWNERS - 1)

    def send(buf, src, dst, send_sem, recv_sem, rel):
        return pltpu.make_async_remote_copy(
            src_ref=buf.at[src], dst_ref=buf.at[dst], send_sem=send_sem, recv_sem=recv_sem.at[dst],
            device_id={"row": device(*rel)}, device_id_type=MESH)

    def send_own(buf, send_sems, recv_sems, rel):
        dz, dy, dc = rel
        return send(buf, 0, SLOT[dz, -dy % 4, dc], send_sems.at[SLOT[rel]], recv_sems, rel)

    def forward(j):
        dz, dy, _ = ORDER[j]
        return send(blk, j, SLOT[dz, dy, 1], blk_send.at[SLOT[dz, dy, 1]], blk_recv, (0, 0, 1))

    for rel in ORDER[1:]:
        send_own(pk, pk_send, pk_recv, rel).start()
    for rel in ORDER[1:]:
        if rel[2] == 0 or rel == (0, 0, 1):
            send_own(blk, blk_send, blk_recv, rel).start()

    def wait_block(j):
        dz, dy, dc = ORDER[j]
        send(blk, 0, j, blk_send.at[j], blk_recv, (0, 0, 1)).wait_recv()

    held = jnp.zeros((8, 128), F32)
    every = cand_ref[...] >> shift
    for o in range(OWNERS):
        hit = jnp.where(every == o, 1.0, 0.0).reshape(8, 8, 128).sum(axis=1)
        held = jnp.where(iota((8, 128), 1) == o, jnp.sum(hit, axis=1, keepdims=True), held)
    lane = iota((128, 128), 1)
    limits = [(hi, last, 1) for _, hi, _, last in TILES[:-1]] + [(lo, first, 0) for lo, _, first, _ in TILES[1:]]
    which = lane >> 4
    window = jnp.zeros((128, 128), jnp.int32)
    for k, (_, edge, _) in enumerate(limits):
        window = jnp.where(which == k, edge, window)
    prefix = ones_where((order_of(iota((128, 128), 0), lane & 15) < window) & (iota((128, 128), 0) < OWNERS))
    sums = dot(held.astype(BF16), prefix)
    bad = held > CAP
    for k, (bound, _, least) in enumerate(limits):
        off = sums < bound if least else sums > bound
        bad = bad | ((which[:8] == k) & off)
    pick_col = pick_col_ref[...] >> shift
    pick_hit = jnp.where(pick_col == iota((PICKS, 128), 1), 1.0, 0.0)
    pick_over = jnp.sum(pick_hit, axis=0, keepdims=True) > PCAP
    worst = jnp.maximum(jnp.max(jnp.where(bad, 1.0, 0.0)), jnp.max(jnp.where(pick_over, 1.0, 0.0)))
    flag_ref[0, 0] = worst.astype(jnp.int32)

    pick_order = order_of(pick_col, me)
    pick_one = ones_where(pick_order == iota((PICKS, 128), 1))
    earlier = dot(ones_where(iota((PICKS, PICKS), 1) < iota((PICKS, PICKS), 0)), pick_one)
    pick_rank_col = jnp.sum(jnp.where(pick_order == iota((PICKS, 128), 1), earlier, 0.0), axis=1, keepdims=True)
    pick_slot = pick_order[:, :1] * PCAP + pick_rank_col.astype(jnp.int32)
    for j in range(1, OWNERS):
        send(pk, 0, j, pk_send.at[j], pk_recv, (0, 0, 1)).wait_recv()
    picked = dot(
        ones_where(pick_slot == iota((PICKS, OWNERS * PCAP), 1)),
        pk[...].reshape(OWNERS * PCAP, emb.shape[1]))
    ch[:PICKS] = picked.astype(BF16)

    seen = {0}
    for t, (lo, hi, first, last) in enumerate(TILES):
        for j in range(last):
            if j not in seen and ORDER[j][2] == 0:
                wait_block(j)
                forward(j).start()
        for j in range(last):
            if j not in seen and ORDER[j][2] == 1:
                wait_block(j)
            seen.add(j)
        dense = jnp.zeros((hi - lo, emb.shape[1]), F32)
        for j in range(first, last):
            row = iota((hi - lo, CAP), 0) + lo
            slot = iota((hi - lo, CAP), 1)
            start = base[8 * j:8 * j + 1, :CAP].astype(jnp.int32)
            held_j = count[8 * j:8 * j + 1, :CAP].astype(jnp.int32)
            dense += dot(ones_where((row == start + slot) & (slot < held_j)), blk[j])
        ch[PICKS + lo:PICKS + hi] = dense.astype(BF16)
        acc[lo:hi] = jnp.zeros((hi - lo, 128), F32)

        def step(i, carry, t=t, lo=lo, hi=hi):
            e = emb[pl.ds(pl.multiple_of(i * block_rows, block_rows), block_rows), :]
            if t == 0:
                s = inner(ch[:PICKS + hi], e)
                cover = jnp.max(s[:PICKS], axis=0, keepdims=True)
                s = s[PICKS:]
            else:
                s = inner(ch[PICKS + lo:PICKS + hi], e)
            part = acc[lo:hi]
            for k in range(block_rows // 128):
                at = pl.ds(i * (block_rows // 128) + k, 1)
                lanes_k = slice(128 * k, 128 * k + 128)
                if t == 0:
                    cover_k = cover[:, lanes_k]
                    cover_ref[at, :] = cover_k
                else:
                    cover_k = cover_ref[at, :]
                part += jnp.maximum(s[:, lanes_k] - cover_k, 0.0)
            acc[lo:hi] = part
            return carry

        lax.fori_loop(0, rows // block_rows, step, 0)

    found = jnp.sum(acc[...], axis=1, keepdims=True)
    dense_at = iota((PER, 128), 0).astype(F32)
    parts = []
    for r in range(8):
        parts.append(jnp.sum(jnp.where(dense_at == place[r:r + 1], found, 0.0), axis=0, keepdims=True))
    red[me] = jnp.concatenate(parts, axis=0)

    def share(rel):
        return pltpu.make_async_remote_copy(
            src_ref=red.at[me], dst_ref=red.at[me], send_sem=red_send.at[SLOT[rel]], recv_sem=red_recv.at[me],
            device_id={"row": device(*rel)}, device_id_type=MESH)

    for rel in ORDER[1:]:
        share(rel).start()
    for rel in ORDER[1:]:
        o = device(*rel)
        pltpu.make_async_remote_copy(
            src_ref=red.at[me], dst_ref=red.at[o], send_sem=red_send.at[SLOT[rel]], recv_sem=red_recv.at[o],
            device_id={"row": o}, device_id_type=MESH).wait_recv()
    whole = red[0]
    for o in range(1, OWNERS):
        whole += red[o]
    gains_ref[...] = whole * (1.0 / (rows * OWNERS))

    for rel in ORDER[1:]:
        send_own(pk, pk_send, pk_recv, rel).wait_send()
        share(rel).wait_send()
        if rel[2] == 0 or rel == (0, 0, 1):
            send_own(blk, blk_send, blk_recv, rel).wait_send()
        if rel[2] == 0:
            forward(SLOT[rel]).wait_send()


def select_owned(embeddings, indices):
    count = embeddings.shape[0]
    local = indices - lax.axis_index("row") * count
    owned = (local >= 0) & (local < count)
    taken = jnp.take(embeddings, jnp.clip(local, 0, count - 1), axis=0)
    return jnp.where(owned[:, None], taken, jnp.zeros_like(taken))


def whole_path(embeddings, pick_index, cand_index):
    count = embeddings.shape[0]
    per = cand_index.shape[0] // lax.axis_size("cand")
    mine = lax.dynamic_slice_in_dim(cand_index, lax.axis_index("cand") * per, per, 0)
    picked = lax.psum(select_owned(embeddings, pick_index), "row")
    coverage = jnp.max(inner(embeddings, picked), axis=1)
    chosen = lax.psum(select_owned(embeddings, mine), "row")
    similar = inner(embeddings, chosen)
    partial = jnp.sum(jnp.maximum(similar - coverage[:, None], 0.0), axis=0)
    return lax.psum(partial, "row") / (count * lax.axis_size("row")), coverage


def per_device(embeddings, pick_index, cand_index):
    rows, width = embeddings.shape
    shift = rows.bit_length() - 1
    chunks = 8
    block_rows = 2048
    pick_row = jnp.concatenate([pick_index, jnp.full((128 - PICKS,), -1, jnp.int32)]).reshape(1, 128)
    vmem = pl.BlockSpec(memory_space=pltpu.VMEM)
    gains, cover, flag = pl.pallas_call(
        functools.partial(kernel, block_rows, shift),
        out_shape=[
            jax.ShapeDtypeStruct((8, 128), F32),
            jax.ShapeDtypeStruct((rows // 128, 128), F32),
            jax.ShapeDtypeStruct((1, 1), jnp.int32),
        ],
        in_specs=[vmem, vmem, vmem, pl.BlockSpec(memory_space=pl.ANY)],
        out_specs=[vmem, vmem, pl.BlockSpec(memory_space=pltpu.SMEM)],
        scratch_shapes=[
            pltpu.VMEM((rows, width), BF16),
            pltpu.VMEM((OWNERS, CAP, width), BF16),
            pltpu.VMEM((OWNERS, PCAP, width), BF16),
            pltpu.VMEM((PICKS + PER, width), BF16),
            pltpu.VMEM((PER, 128), F32),
            pltpu.VMEM((OWNERS, 8, 128), F32),
            pltpu.SemaphoreType.DMA((chunks,)),
            pltpu.SemaphoreType.DMA((OWNERS,)),
            pltpu.SemaphoreType.DMA((OWNERS,)),
            pltpu.SemaphoreType.DMA((OWNERS,)),
            pltpu.SemaphoreType.DMA((OWNERS,)),
            pltpu.SemaphoreType.DMA((OWNERS,)),
            pltpu.SemaphoreType.DMA((OWNERS,)),
        ],
        compiler_params=pltpu.CompilerParams(
            collective_id=0, has_side_effects=True, vmem_limit_bytes=60 * 2**20),
        cost_estimate=pl.CostEstimate(
            flops=2 * rows * (PER + PICKS) * width, bytes_accessed=2 * rows * width, transcendentals=0),
    )(cand_index.reshape(-1, 128), pick_row, pick_index.reshape(PICKS, 1), embeddings)
    return lax.cond(
        flag[0, 0] == 0,
        lambda: (gains.reshape(PER), cover.reshape(rows)),
        lambda: whole_path(embeddings, pick_index, cand_index),
    )


def solution(mesh):
    return jax.shard_map(
        per_device,
        mesh=mesh,
        in_specs=(P("row", None), P(), P()),
        out_specs=(P("cand"), P("row")),
        check_vma=False,
    )
```

time: 299 us -> 76.2 us (0.25)
  waiting for transfers between devices: 162 us -> 0 us
  Pallas kernels: 0 us -> 56.6 us
  local copies, waits for them, and re-layouts: 50.2 us -> 4.5 us
  blocking collectives: 28.6 us -> 0 us
  matrix products: 25.3 us -> 0 us
  other arithmetic: 16.6 us -> 0 us
    psum x1 -> x0, waiting for transfers between devices: 162 us -> none  [per_device(): lax.psum(select_owned(embeddings, pick_index), 'row').astype(jnp.float32)]
    pallas_call x0 -> x1, Pallas kernels: none -> 56.6 us  [per_device(): pl.pallas_call(functools.partial(kernel, block_rows, shift), out_shape=[j...]
    gather x2 -> x0, local copies, waits for them, and re-layouts: 50.2 us -> none  [select_owned(): taken = jnp.take(embeddings, jnp.clip(local, 0, count - 1), axis=0)]
    psum x1 -> x0, blocking collectives: 28.6 us -> none  [per_device(): gains = lax.psum(partial_gain, 'row') / total_rows]
    dot_general x2 -> x0, matrix products: 25.3 us -> none  [inner(): lax.dot_general(left, right, (((1,), (1,)), ((), ())), preferred_element_...]
    select_n x2 -> x0, other arithmetic: 13.8 us -> none  [select_owned(): return jnp.where(owned[:, None], taken, jnp.zeros_like(taken))]
  transfers between devices with their start and end apart: 1 -> 0, of which waited for: 1 -> 0; matrix products, arithmetic and copies ran while one was open for 0% -> 0% of each run, Pallas kernels for 0% -> 0%
where the time goes in v1:
time: 76.2 us; the launch traced here: 76 us
  Pallas kernels  56.6 us (74%)
  between operations  14.7 us (19%)
  local copies, waits for them, and re-layouts  4.5 us (6%)
    pallas_call x1, Pallas kernels, per_device(): pl.pallas_call(functools.partial(kernel, block_rows, shift), out_shape=[j...  56.6 us
    unnamed x4, local copies, waits for them, and re-layouts  1.97 us

profile of v1, /device:TPU:1, one launch (start us, length us, event | category | flops | bytes accessed | tf_op | source)
XLA Modules:
  0.0 76.0 jit_solution(6043370468779570193)
XLA Ops:
  7.2 1.2 %pad_bitcast_fusion.pick_ref = s32[1,128]{1,0:T(1,128)} fusion(s32[64]{0:T(128)} %param.6), kind=kLoop, calls=%fused_computation.16 | loop fusion | bytes 768 | tf_op jit(solution)/shard_map/reshape | solution.py:286
  8.3 1.4 %copy.7.pick_col_ref = s32[64,1]{1,0:T(8,128)} copy(s32[64,1]{0,1:T(1,128)} %bitcast.12) | data formatting | bytes 512 | tf_op jit(solution)/shard_map/reshape | solution.py:316
  9.7 0.0 copy-start
  9.7 56.6 %shard_map.52 = (f32[8,128]{1,0:T(8,128)S(1)}, f32[64,128]{1,0:T(8,128)}, s32[1,1]{1,0:T(1,128)}) custom-call(s32[64,128]{1,0:T(8,128)} %bitcast.13, s32[1,128]{1,0:T(1,128)} %pad_bitcast_fusion.pick_ref, s32[64,1]{1,0:T(8,128)} %copy.7.pick_col_ref, bf16[8192,768]{1,0:T(8,128)(2,1)} %emb_hbm.1), custom_call_target="tpu_custom_call" | custom-call | flops 13690208256 | bytes 12582912 | tf_op jit(solution)/shard_map/pallas_call | solution.py:288
  66.9 0.0 copy-done
  66.9 0.2 conditional.1
  67.1 0.6 copy.16
  67.7 1.4 %copy.17 = f32[8192]{0:T(1024)} copy(f32[8192]{0:T(1024)} %get-tuple-element.38) | data formatting | bytes 65536
Async XLA Ops:
  9.7 57.2 %copy-start = (s32[64]{0:T(128)S(1)}, s32[64]{0:T(128)}, u32[]{:S(2)}) copy-start(s32[64]{0:T(128)} %param.6) | copy-start | bytes 772

commit v2 on v1

--- a/solution.py
+++ b/solution.py
@@ -266,16 +266,25 @@
     return jnp.where(owned[:, None], taken, jnp.zeros_like(taken))
 
 
+def sum_over_rows(x):
+    size = lax.axis_size("row")
+    step = 1
+    while step < size:
+        x = x + lax.ppermute(x, "row", [(i, i ^ step) for i in range(size)])
+        step *= 2
+    return x
+
+
 def whole_path(embeddings, pick_index, cand_index):
     count = embeddings.shape[0]
     per = cand_index.shape[0] // lax.axis_size("cand")
     mine = lax.dynamic_slice_in_dim(cand_index, lax.axis_index("cand") * per, per, 0)
-    picked = lax.psum(select_owned(embeddings, pick_index), "row")
+    picked = sum_over_rows(select_owned(embeddings, pick_index))
     coverage = jnp.max(inner(embeddings, picked), axis=1)
-    chosen = lax.psum(select_owned(embeddings, mine), "row")
+    chosen = sum_over_rows(select_owned(embeddings, mine))
     similar = inner(embeddings, chosen)
     partial = jnp.sum(jnp.maximum(similar - coverage[:, None], 0.0), axis=0)
-    return lax.psum(partial, "row") / (count * lax.axis_size("row")), coverage
+    return sum_over_rows(partial) / (count * lax.axis_size("row")), coverage
 
 
 def per_device(embeddings, pick_index, cand_index):

time: 76.2 us -> 62.8 us (0.82)
  between operations: 14.7 us -> 1.22 us
where the time goes in v2:
time: 62.8 us; the launch traced here: 62.5 us
  Pallas kernels  56.6 us (90%)
  local copies, waits for them, and re-layouts  4.5 us (7%)
  between operations  1.22 us (2%)
    pallas_call x1, Pallas kernels, per_device(): pl.pallas_call(functools.partial(kernel, block_rows, shift), out_shape=[j...  56.6 us
    unnamed x4, local copies, waits for them, and re-layouts  1.97 us
    reshape x1, local copies, waits for them, and re-layouts, per_device(): pick_index.reshape(PICKS, 1)  1.36 us

profile of v2, /device:TPU:1, one launch (start us, length us, event | category | flops | bytes accessed | tf_op | source)
XLA Modules:
  0.0 62.5 jit_solution(14668622762924761812)
XLA Ops:
  0.6 1.2 %pad_bitcast_fusion.pick_ref = s32[1,128]{1,0:T(1,128)} fusion(s32[64]{0:T(128)} %param.6), kind=kLoop, calls=%fused_computation.18 | loop fusion | bytes 768 | tf_op jit(solution)/shard_map/reshape | solution.py:295
  1.8 1.4 %copy.7.pick_col_ref = s32[64,1]{1,0:T(8,128)} copy(s32[64,1]{0,1:T(1,128)} %bitcast.10) | data formatting | bytes 512 | tf_op jit(solution)/shard_map/reshape | solution.py:325
  3.2 0.0 copy-start
  3.2 56.6 %shard_map.52 = (f32[8,128]{1,0:T(8,128)S(1)}, f32[64,128]{1,0:T(8,128)}, s32[1,1]{1,0:T(1,128)}) custom-call(s32[64,128]{1,0:T(8,128)} %bitcast.11, s32[1,128]{1,0:T(1,128)} %pad_bitcast_fusion.pick_ref, s32[64,1]{1,0:T(8,128)} %copy.7.pick_col_ref, bf16[8192,768]{1,0:T(8,128)(2,1)} %emb_hbm.1), custom_call_target="tpu_custom_call" | custom-call | flops 13690208256 | bytes 12582912 | tf_op jit(solution)/shard_map/pallas_call | solution.py:297
  60.3 0.0 copy-done
  60.3 0.2 conditional.1
  60.5 0.6 copy.14
  61.1 1.4 %copy.15 = f32[8192]{0:T(1024)} copy(f32[8192]{0:T(1024)} %get-tuple-element.36) | data formatting | bytes 65536
Async XLA Ops:
  3.2 57.1 %copy-start = (s32[64]{0:T(128)S(1)}, s32[64]{0:T(128)}, u32[]{:S(2)}) copy-start(s32[64]{0:T(128)} %param.6) | copy-start | bytes 772

commit v3 on v2

v3 whole, which is shorter than its diff:
```python
import functools

import jax
import jax.numpy as jnp
from jax import lax
from jax.experimental import pallas as pl
from jax.experimental.pallas import tpu as pltpu
from jax.sharding import PartitionSpec as P

MESH = pl.DeviceIdType.MESH
F32 = jnp.float32
BF16 = jnp.bfloat16

CHIPS = ((0, 0), (1, 0), (0, 1), (0, 3), (1, 1), (1, 3), (0, 2), (1, 2))
ORDER = tuple((dz, dy, dc) for dz, dy in CHIPS for dc in (0, 1))
SLOT = {rel: j for j, rel in enumerate(ORDER)}
OWNERS = 16
PER = 1024
PICKS = 64
PCAP = 16
UNIT = 48
REST = 272
PICK_AT = 2 * UNIT
REST_AT = OWNERS * UNIT + PICKS
STREAM = REST_AT + REST
PASSES = ((0, 96, 4096), (96, 448, 2048), (448, 640, 4096), (640, STREAM, 2048))


def unit_at(j):
    return UNIT * j + (PICKS if j >= 2 else 0)


def iota(shape, dim):
    return lax.broadcasted_iota(jnp.int32, shape, dim)


def dot(a, b):
    return jnp.dot(a, b, preferred_element_type=F32)


def inner(left, right):
    return lax.dot_general(left, right, (((1,), (1,)), ((), ())), preferred_element_type=F32)


def ones_where(cond):
    return jnp.where(cond, 1.0, 0.0).astype(BF16)


def order_of(owner, device):
    dz = (owner >> 3) ^ (device >> 3)
    dy = ((owner >> 1) - (device >> 1)) & 3
    chip = dz * 4 + dy
    place = jnp.zeros_like(chip)
    for rank, (cz, cy) in enumerate(CHIPS):
        place = jnp.where(chip == cz * 4 + cy, rank, place)
    return place * 2 + ((owner ^ device) & 1)


def kernel(
    shift,
    cand_hbm, pick_hbm, emb_hbm,
    gains_ref, cover_hbm, flag_ref,
    cand_ref, pick_ref, emb, ch, late, pk, raw, cover_ref, acc, red,
    in_sem, load_sem, pk_send, pk_recv, ch_send, ch_recv, late_send, late_recv, red_send, red_recv,
):
    rows = emb.shape[0]
    width = emb.shape[1]
    chunks = load_sem.shape[0]
    chunk = rows // chunks
    me = lax.axis_index("row")
    group = lax.axis_index("cand")
    z, y, c = me // 8, (me // 2) % 4, me % 2

    def device(dz, dy, dc):
        return (z + dz) % 2 * 8 + (y + dy) % 4 * 2 + (c + dc) % 2

    def load(i):
        at = pl.ds(pl.multiple_of(i * chunk, chunk), chunk)
        return pltpu.make_async_copy(emb_hbm.at[at], emb.at[at], load_sem.at[i])

    cand_in = pltpu.make_async_copy(cand_hbm, cand_ref, in_sem.at[0])
    pick_in = pltpu.make_async_copy(pick_hbm, pick_ref, in_sem.at[1])
    cover_out = pltpu.make_async_copy(cover_ref, cover_hbm, in_sem.at[2])
    cand_in.start()
    pick_in.start()
    for i in range(chunks):
        load(i).start()

    barrier = pltpu.get_barrier_semaphore()
    for rel in ORDER[1:]:
        pl.semaphore_signal(barrier, inc=1, device_id={"row": device(*rel)}, device_id_type=MESH)
    cand_in.wait()
    pick_in.wait()

    mine = cand_ref[pl.ds(pl.multiple_of(group * 8, 8), 8), :]
    owner, local = mine >> shift, mine & (rows - 1)
    masks = [owner == device(*rel) for rel in ORDER]
    mask = jnp.concatenate([jnp.where(m, 1.0, 0.0) for m in masks], axis=0).astype(BF16)
    r0, r1 = iota((128, 128), 0), iota((128, 128), 1)
    before = ones_where(r0 < r1)
    within = dot(mask, before)
    totals = dot(mask, jnp.ones((128, 128), BF16)).astype(BF16)
    same = (r0 >> 3) == (r1 >> 3)
    rank = within + dot(ones_where(same & (r1 < r0)), totals)

    slots = iota((2 * UNIT, 128), 0).astype(F32)
    key = jnp.where(masks[0], rank[:8], -1.0)
    local_plus = (local + 1).astype(F32)
    slot_row = jnp.zeros((2 * UNIT, 128), F32)
    for r in range(8):
        slot_row += jnp.where(slots == key[r:r + 1], local_plus[r:r + 1], 0.0)
    cand_at = jnp.sum(slot_row, axis=1, keepdims=True)
    pick = pick_ref[...]
    pick_mine = (pick >> shift) == me
    pick_rank = dot(ones_where(jnp.broadcast_to(pick_mine, (8, PICKS))), before[:PICKS, :PICKS])
    pick_key = jnp.where(pick_mine, pick_rank[:1], -1.0)
    pick_plus = ((pick & (rows - 1)) + 1).astype(F32)
    pick_at = jnp.sum(
        jnp.where(iota((PCAP, PICKS), 0).astype(F32) == pick_key, pick_plus, 0.0), axis=1, keepdims=True)
    held_rows = 2 * UNIT + PCAP
    at_row = jnp.concatenate([cand_at, pick_at], axis=0).astype(jnp.int32) - 1
    at_row = jnp.broadcast_to(at_row, (held_rows, chunk))

    lanes = iota((held_rows, chunk), 1)

    def gather(i, total):
        load(i).wait()
        at = pl.ds(pl.multiple_of(i * chunk, chunk), chunk)
        return total + dot(ones_where(at_row - i * chunk == lanes), emb[at, :])

    total = lax.fori_loop(0, chunks, gather, jnp.zeros((held_rows, width), F32))
    pk[0] = total[2 * UNIT:].astype(BF16)
    ch[:UNIT] = total[:UNIT].astype(BF16)
    late[0] = total[UNIT:2 * UNIT].astype(BF16)

    pl.semaphore_wait(barrier, OWNERS - 1)

    def remote(src, dst, send_sem, recv_sem, to):
        return pltpu.make_async_remote_copy(
            src_ref=src, dst_ref=dst, send_sem=send_sem, recv_sem=recv_sem,
            device_id={"row": to}, device_id_type=MESH)

    def ch_block(j):
        return ch.at[pl.ds(unit_at(j), UNIT)]

    def late_block(j):
        return late.at[j]

    def pk_block(j):
        return pk.at[j]

    CH = (ch_block, ch_send, ch_recv)
    LATE = (late_block, late_send, late_recv)
    PK = (pk_block, pk_send, pk_recv)

    def own(part, rel):
        block, sent, got = part
        dz, dy, dc = rel
        to = SLOT[dz, -dy % 4, dc]
        return remote(block(0), block(to), sent.at[SLOT[rel]], got.at[to], device(*rel))

    def hand(part, chip):
        block, sent, got = part
        j = SLOT[(*chip, 0)]
        return remote(block(j), block(j + 1), sent.at[j + 1], got.at[j + 1], device(0, 0, 1))

    def relay(part, dz):
        block, sent, got = part
        to = SLOT[dz, 2, 0]
        first = SLOT[dz, 3, 0] - 2 * c
        if part is CH:
            src = ch.at[pl.ds(pl.multiple_of(first * UNIT + PICKS, 16), UNIT)]
        else:
            src = block(first)
        return remote(src, block(to), sent.at[to], got.at[to], device(0, 1 + 2 * c, 0))

    def arrived(part, *js):
        block, sent, got = part
        for j in js:
            remote(block(0), block(j), sent.at[j], got.at[j], device(0, 0, 1)).wait_recv()

    SIB = (0, 0, 1)
    NEAR = ((1, 0), (0, 1), (0, 3))
    DIAG = ((1, 1), (1, 3))
    FAR = ((0, 2), (1, 2))

    def evens(chips):
        return [SLOT[(*chip, 0)] for chip in chips]

    def odds(chips):
        return [SLOT[(*chip, 1)] for chip in chips]

    own(PK, SIB).start()
    for chip in FAR + DIAG + NEAR:
        own(PK, (*chip, 0)).start()
    own(CH, SIB).start()
    for chip in NEAR + DIAG:
        own(CH, (*chip, 0)).start()

    held = jnp.zeros((8, 128), F32)
    every = cand_ref[...] >> shift
    lane8 = iota((8, 128), 1)
    for o in range(OWNERS):
        hit = jnp.where(every == o, 1.0, 0.0).reshape(8, 8, 128).sum(axis=1)
        held = jnp.where(lane8 == o, jnp.sum(hit, axis=1, keepdims=True), held)
    over = jnp.maximum(held - UNIT, 0.0)
    bad = (over > UNIT) | (jnp.sum(over, axis=1, keepdims=True) > REST)
    eye = iota((PICKS, PICKS), 0) == iota((PICKS, PICKS), 1)
    pick_col = jnp.sum(jnp.where(eye, (pick >> shift).astype(F32), 0.0), axis=1, keepdims=True).astype(jnp.int32)
    pick_hit = jnp.where(pick_col == iota((PICKS, 128), 1), 1.0, 0.0)
    pick_over = jnp.sum(pick_hit, axis=0, keepdims=True) > PCAP
    worst = jnp.maximum(jnp.max(jnp.where(bad, 1.0, 0.0)), jnp.max(jnp.where(pick_over, 1.0, 0.0)))
    flag_ref[0, 0] = worst.astype(jnp.int32)

    count = dot(ones_where(same), totals)
    rest = jnp.maximum(count - UNIT, 0.0).astype(BF16)
    rest_base = dot(ones_where(((r1 >> 3) < (r0 >> 3)) & ((r1 & 7) == 0)), rest)
    place = jnp.zeros((8, 128), F32)
    for j in range(OWNERS):
        at = slice(8 * j, 8 * j + 8)
        row = jnp.where(rank[at] < UNIT, rank[at] + unit_at(j), rank[at] + (rest_base[at] + (REST_AT - UNIT)))
        place += jnp.where(masks[j], row, 0.0)

    pick_order = order_of(pick_col, me)
    pick_one = ones_where(pick_order == iota((PICKS, 128), 1))
    earlier = dot(ones_where(iota((PICKS, PICKS), 1) < iota((PICKS, PICKS), 0)), pick_one)
    pick_rank_col = jnp.sum(jnp.where(pick_order == iota((PICKS, 128), 1), earlier, 0.0), axis=1, keepdims=True)
    pick_slot = pick_order * PCAP + pick_rank_col.astype(jnp.int32)
    pick_pack = ones_where(pick_slot == iota((PICKS, OWNERS * PCAP), 1))
    group_over = jnp.where(iota((8, 128), 0) == group, over, 0.0).astype(BF16)
    late_slots = OWNERS * UNIT
    block_of = (iota((128, late_slots), 1) * 1366) >> 16
    order_col = order_of(iota((128, late_slots), 0), me)
    order_col = jnp.where(iota((128, late_slots), 0) < OWNERS, order_col, OWNERS)
    late_base = jnp.sum(dot(group_over, ones_where(order_col < block_of)), axis=0, keepdims=True)
    late_count = jnp.sum(dot(group_over, ones_where(order_col == block_of)), axis=0, keepdims=True)
    late_slot = (iota((1, late_slots), 1) - block_of[:1] * UNIT).astype(F32)
    late_row = jnp.where(late_slot < late_count, late_base + late_slot, -1.0)

    def one_pass(t, polls):
        lo, hi, step_rows = PASSES[t]
        acc[lo:hi] = jnp.zeros((hi - lo, 128), F32)
        groups = step_rows // 128

        def step(i, carry):
            e = emb[pl.ds(pl.multiple_of(i * step_rows, step_rows), step_rows), :]
            s = inner(ch[lo:hi], e)
            if t == 0:
                raw[:, pl.ds(pl.multiple_of(i * step_rows, step_rows), step_rows)] = s
            else:
                if t == 1:
                    cover = jnp.max(s[:PICKS], axis=0, keepdims=True)
                    s = s[PICKS:]
                    held_back = acc[:PICK_AT]
                at_acc = lo + PICKS if t == 1 else lo
                part = acc[at_acc:hi]
                for k in range(groups):
                    at = pl.ds(i * groups + k, 1)
                    lanes_k = slice(128 * k, 128 * k + 128)
                    if t == 1:
                        cover_k = cover[:, lanes_k]
                        cover_ref[at, :] = cover_k
                        raw_k = raw[:, pl.ds(pl.multiple_of(i * step_rows + 128 * k, 128), 128)]
                        held_back += jnp.maximum(raw_k - cover_k, 0.0)
                    else:
                        cover_k = cover_ref[at, :]
                    part += jnp.maximum(s[:, lanes_k] - cover_k, 0.0)
                acc[at_acc:hi] = part
                if t == 1:
                    acc[:PICK_AT] = held_back
            for n, poll in polls.items():
                pl.when(i == n)(poll)
            return carry

        lax.fori_loop(0, rows // step_rows, step, 0)

    def hand_all(part, chips):
        arrived(part, *evens(chips))
        for chip in chips:
            hand(part, chip).start()

    def near(part):
        hand_all(part, NEAR)
        relay(part, 0).start()

    def diagonal(part):
        hand_all(part, DIAG)
        relay(part, 1).start()

    def far(part):
        hand_all(part, FAR)

    def send_late():
        own(LATE, SIB).start()
        for chip in NEAR + DIAG:
            own(LATE, (*chip, 0)).start()

    arrived(CH, SLOT[SIB])
    one_pass(0, {0: lambda: hand_all(PK, NEAR)})
    hand_all(PK, DIAG)
    near(CH)
    hand_all(PK, FAR)
    arrived(PK, *range(1, OWNERS, 2))
    send_late()
    ch[PICK_AT:PICK_AT + PICKS] = dot(pick_pack, pk[...].reshape(OWNERS * PCAP, width)).astype(BF16)
    arrived(CH, *odds(NEAR))
    acc[:PICK_AT] = jnp.zeros((PICK_AT, 128), F32)
    one_pass(1, {0: lambda: diagonal(CH), 1: lambda: far(CH), 2: lambda: near(LATE)})
    cover_out.start()
    arrived(CH, *odds(DIAG))
    one_pass(2, {0: lambda: diagonal(LATE)})
    far(LATE)
    arrived(CH, *odds(FAR))
    arrived(LATE, *range(1, OWNERS, 2))
    packed = dot(ones_where(iota((REST, late_slots), 0).astype(F32) == late_row), late[...].reshape(late_slots, width))
    ch[REST_AT:] = packed.astype(BF16)
    one_pass(3, {})

    found = jnp.sum(acc[...], axis=1, keepdims=True)
    dense_at = iota((STREAM, 128), 0).astype(F32)
    parts = []
    for r in range(8):
        parts.append(jnp.sum(jnp.where(dense_at == place[r:r + 1], found, 0.0), axis=0, keepdims=True))
    red[me] = jnp.concatenate(parts, axis=0)

    def share(rel, at):
        return remote(red.at[me], red.at[at], red_send.at[SLOT[rel]], red_recv.at[at], device(*rel))

    for rel in ORDER[:0:-1]:
        share(rel, me).start()
    for rel in ORDER[1:]:
        share(rel, device(*rel)).wait_recv()
    whole = red[0]
    for o in range(1, OWNERS):
        whole += red[o]
    gains_ref[...] = whole * (1.0 / (rows * OWNERS))

    cover_out.wait()
    for rel in ORDER[1:]:
        share(rel, me).wait_send()
    for part in (PK, CH, LATE):
        own(part, SIB).wait_send()
        for chip in NEAR + DIAG:
            own(part, (*chip, 0)).wait_send()
            hand(part, chip).wait_send()
        for chip in FAR:
            if part is PK:
                own(part, (*chip, 0)).wait_send()
            else:
                relay(part, chip[0]).wait_send()
            hand(part, chip).wait_send()


def select_owned(embeddings, indices):
    count = embeddings.shape[0]
    local = indices - lax.axis_index("row") * count
    owned = (local >= 0) & (local < count)
    taken = jnp.take(embeddings, jnp.clip(local, 0, count - 1), axis=0)
    return jnp.where(owned[:, None], taken, jnp.zeros_like(taken))


def sum_over_rows(x):
    size = lax.axis_size("row")
    step = 1
    while step < size:
        x = x + lax.ppermute(x, "row", [(i, i ^ step) for i in range(size)])
        step *= 2
    return x


def whole_path(embeddings, pick_index, cand_index):
    count = embeddings.shape[0]
    per = cand_index.shape[0] // lax.axis_size("cand")
    mine = lax.dynamic_slice_in_dim(cand_index, lax.axis_index("cand") * per, per, 0)
    picked = sum_over_rows(select_owned(embeddings, pick_index))
    coverage = jnp.max(inner(embeddings, picked), axis=1)
    chosen = sum_over_rows(select_owned(embeddings, mine))
    similar = inner(embeddings, chosen)
    partial = jnp.sum(jnp.maximum(similar - coverage[:, None], 0.0), axis=0)
    return sum_over_rows(partial) / (count * lax.axis_size("row")), coverage


def per_device(embeddings, pick_index, cand_index):
    rows, width = embeddings.shape
    shift = rows.bit_length() - 1
    chunks = 8
    anywhere = pl.BlockSpec(memory_space=pl.ANY)
    dma = pltpu.SemaphoreType.DMA
    gains, cover, flag = pl.pallas_call(
        functools.partial(kernel, shift),
        out_shape=[
            jax.ShapeDtypeStruct((8, 128), F32),
            jax.ShapeDtypeStruct((rows // 128, 128), F32),
            jax.ShapeDtypeStruct((1, 1), jnp.int32),
        ],
        in_specs=[anywhere, anywhere, anywhere],
        out_specs=[pl.BlockSpec(memory_space=pltpu.VMEM), anywhere, pl.BlockSpec(memory_space=pltpu.SMEM)],
        scratch_shapes=[
            pltpu.VMEM((64, 128), jnp.int32),
            pltpu.VMEM((1, PICKS), jnp.int32),
            pltpu.VMEM((rows, width), BF16),
            pltpu.VMEM((STREAM, width), BF16),
            pltpu.VMEM((OWNERS, UNIT, width), BF16),
            pltpu.VMEM((OWNERS, PCAP, width), BF16),
            pltpu.VMEM((2 * UNIT, rows), F32),
            pltpu.VMEM((rows // 128, 128), F32),
            pltpu.VMEM((STREAM, 128), F32),
            pltpu.VMEM((OWNERS, 8, 128), F32),
            dma((3,)), dma((chunks,)),
        ] + [dma((OWNERS,))] * 8,
        compiler_params=pltpu.CompilerParams(
            collective_id=0, has_side_effects=True, vmem_limit_bytes=60 * 2**20),
        cost_estimate=pl.CostEstimate(
            flops=2 * rows * (PER + PICKS) * width, bytes_accessed=2 * rows * width, transcendentals=0),
    )(cand_index.reshape(-1, 128), pick_index.reshape(1, PICKS), embeddings)
    return lax.cond(
        flag[0, 0] == 0,
        lambda: (gains.reshape(PER), cover.reshape(rows)),
        lambda: whole_path(embeddings, pick_index, cand_index),
    )


def solution(mesh):
    return jax.shard_map(
        per_device,
        mesh=mesh,
        in_specs=(P("row", None), P(), P()),
        out_specs=(P("cand"), P("row")),
        check_vma=False,
    )
```

time: 62.8 us -> 52.7 us (0.84)
  Pallas kernels: 56.6 us -> 49.1 us
  local copies, waits for them, and re-layouts: 4.5 us -> 1.97 us
    pallas_call x1, Pallas kernels: 56.6 us -> 49.1 us  [per_device(): pl.pallas_call(functools.partial(kernel, shift), out_shape=[jax.ShapeDtyp...]
    reshape x2 -> x0, local copies, waits for them, and re-layouts: 2.53 us -> none  [the longest x1 1.36 us: per_device(): pick_index.reshape(PICKS, 1)]
where the time goes in v3:
time: 52.7 us; the launch traced here: 52.6 us
  Pallas kernels  49.1 us (93%)
  local copies, waits for them, and re-layouts  1.97 us (4%)
  between operations  1.22 us (2%)
    pallas_call x1, Pallas kernels, per_device(): pl.pallas_call(functools.partial(kernel, shift), out_shape=[jax.ShapeDtyp...  49.1 us
    unnamed x4, local copies, waits for them, and re-layouts  1.97 us

profile of v3, /device:TPU:1, one launch (start us, length us, event | category | flops | bytes accessed | tf_op | source)
XLA Modules:
  0.0 52.6 jit_solution(1850389586160136527)
XLA Ops:
  0.6 0.0 copy-start
  0.6 49.1 %shard_map.52 = (f32[8,128]{1,0:T(8,128)S(1)}, f32[64,128]{1,0:T(8,128)}, s32[1,1]{1,0:T(1,128)}) custom-call(s32[64,128]{1,0:T(8,128)} %bitcast.8, s32[1,64]{1,0:T(1,128)} %bitcast.9, bf16[8192,768]{1,0:T(8,128)(2,1)} %emb_hbm.1), custom_call_target="tpu_custom_call" | custom-call | flops 13690208256 | bytes 12582912 | tf_op jit(solution)/shard_map/pallas_call | solution.py:389
  50.3 0.0 copy-done
  50.3 0.2 conditional.1
  50.6 0.6 %copy.13 = f32[1024]{0:T(1024)} copy(f32[1024]{0:T(1024)S(1)} %get-tuple-element.35) | data formatting | bytes 8192
  51.2 1.4 %copy.14 = f32[8192]{0:T(1024)} copy(f32[8192]{0:T(1024)} %get-tuple-element.36) | data formatting | bytes 65536
Async XLA Ops:
  0.6 49.7 %copy-start = (s32[64]{0:T(128)S(1)}, s32[64]{0:T(128)}, u32[]{:S(2)}) copy-start(s32[64]{0:T(128)} %param.6) | copy-start | bytes 772

commit v4 on v3

--- a/solution.py
+++ b/solution.py
@@ -23,7 +23,8 @@
 PICK_AT = 2 * UNIT
 REST_AT = OWNERS * UNIT + PICKS
 STREAM = REST_AT + REST
-PASSES = ((0, 96, 4096), (96, 448, 2048), (448, 640, 4096), (640, STREAM, 2048))
+PASSES = ((0, PICK_AT), (PICK_AT, 448), (448, 736), (736, STREAM))
+STEP_ROWS = 2048
 
 
 def unit_at(j):
@@ -164,15 +165,21 @@
         j = SLOT[(*chip, 0)]
         return remote(block(j), block(j + 1), sent.at[j + 1], got.at[j + 1], device(0, 0, 1))
 
+    def moved(part, src, to, device_to):
+        block, sent, got = part
+        if part is CH:
+            ref = ch.at[pl.ds(pl.multiple_of(src * UNIT + PICKS, 16), UNIT)]
+        else:
+            ref = block(src)
+        return remote(ref, block(to), sent.at[to], got.at[to], device_to)
+
     def relay(part, dz):
-        block, sent, got = part
-        to = SLOT[dz, 2, 0]
-        first = SLOT[dz, 3, 0] - 2 * c
-        if part is CH:
-            src = ch.at[pl.ds(pl.multiple_of(first * UNIT + PICKS, 16), UNIT)]
-        else:
-            src = block(first)
-        return remote(src, block(to), sent.at[to], got.at[to], device(0, 1 + 2 * c, 0))
+        return moved(part, SLOT[dz, 3, 0] - 2 * c, SLOT[dz, 2, 0], device(0, 1 + 2 * c, 0))
+
+    def across(part, dy):
+        along_y = SLOT[0, dy, 0]
+        src = along_y - c * (along_y - SLOT[1, 0, 0])
+        return moved(part, src, SLOT[1, dy, 0], device(1 - c, c * (-dy % 4), 0))
 
     def arrived(part, *js):
         block, sent, got = part
@@ -190,12 +197,12 @@
     def odds(chips):
         return [SLOT[(*chip, 1)] for chip in chips]
 
-    own(PK, SIB).start()
+    for chip in NEAR:
+        own(CH, (*chip, 0)).start()
+    own(CH, SIB).start()
     for chip in FAR + DIAG + NEAR:
         own(PK, (*chip, 0)).start()
-    own(CH, SIB).start()
-    for chip in NEAR + DIAG:
-        own(CH, (*chip, 0)).start()
+    own(PK, SIB).start()
 
     held = jnp.zeros((8, 128), F32)
     every = cand_ref[...] >> shift
@@ -237,42 +244,48 @@
     late_slot = (iota((1, late_slots), 1) - block_of[:1] * UNIT).astype(F32)
     late_row = jnp.where(late_slot < late_count, late_base + late_slot, -1.0)
 
+    def gain_of(get, covers, lo, hi):
+        for top in range(lo, hi, 64):
+            end = min(top + 64, hi)
+            part = acc[top:end]
+            for k, cover in enumerate(covers):
+                part += jnp.maximum(get(top, end, k) - cover, 0.0)
+            acc[top:end] = part
+
     def one_pass(t, polls):
-        lo, hi, step_rows = PASSES[t]
-        acc[lo:hi] = jnp.zeros((hi - lo, 128), F32)
-        groups = step_rows // 128
+        lo, hi = PASSES[t]
+        groups = STEP_ROWS // 128
 
         def step(i, carry):
-            e = emb[pl.ds(pl.multiple_of(i * step_rows, step_rows), step_rows), :]
-            s = inner(ch[lo:hi], e)
+            at = pl.multiple_of(i * STEP_ROWS, STEP_ROWS)
+            s = inner(ch[lo:hi], emb[pl.ds(at, STEP_ROWS), :])
+
+            def kept(top, end, k):
+                return raw[top:end, pl.ds(pl.multiple_of(at + 128 * k, 128), 128)]
+
+            def new(top, end, k):
+                return s[top - lo:end - lo, 128 * k:128 * k + 128]
+
             if t == 0:
-                raw[:, pl.ds(pl.multiple_of(i * step_rows, step_rows), step_rows)] = s
+                raw[:, pl.ds(at, STEP_ROWS)] = s
+            elif t == 1:
+                cover = jnp.max(s[:PICKS], axis=0, keepdims=True)
+                covers = [cover[:, 128 * k:128 * k + 128] for k in range(groups)]
+                for k in range(groups):
+                    cover_ref[pl.ds(i * groups + k, 1), :] = covers[k]
+                gain_of(kept, covers, 0, PICK_AT)
+                gain_of(new, covers, PICK_AT + PICKS, hi)
             else:
-                if t == 1:
-                    cover = jnp.max(s[:PICKS], axis=0, keepdims=True)
-                    s = s[PICKS:]
-                    held_back = acc[:PICK_AT]
-                at_acc = lo + PICKS if t == 1 else lo
-                part = acc[at_acc:hi]
-                for k in range(groups):
-                    at = pl.ds(i * groups + k, 1)
-                    lanes_k = slice(128 * k, 128 * k + 128)
-                    if t == 1:
-                        cover_k = cover[:, lanes_k]
-                        cover_ref[at, :] = cover_k
-                        raw_k = raw[:, pl.ds(pl.multiple_of(i * step_rows + 128 * k, 128), 128)]
-                        held_back += jnp.maximum(raw_k - cover_k, 0.0)
-                    else:
-                        cover_k = cover_ref[at, :]
-                    part += jnp.maximum(s[:, lanes_k] - cover_k, 0.0)
-                acc[at_acc:hi] = part
-                if t == 1:
-                    acc[:PICK_AT] = held_back
-            for n, poll in polls.items():
-                pl.when(i == n)(poll)
+                covers = [cover_ref[pl.ds(i * groups + k, 1), :] for k in range(groups)]
+                gain_of(new, covers, lo, hi)
+            for n, todo in polls.items():
+                @pl.when(i == n)
+                def _(todo=todo):
+                    for act in todo:
+                        act()
             return carry
 
-        lax.fori_loop(0, rows // step_rows, step, 0)
+        lax.fori_loop(0, rows // STEP_ROWS, step, 0)
 
     def hand_all(part, chips):
         arrived(part, *evens(chips))
@@ -280,37 +293,43 @@
             hand(part, chip).start()
 
     def near(part):
-        hand_all(part, NEAR)
+        arrived(part, *evens(NEAR))
+        for dy in (1, 3):
+            across(part, dy).start()
         relay(part, 0).start()
+        for chip in NEAR:
+            hand(part, chip).start()
 
     def diagonal(part):
-        hand_all(part, DIAG)
+        arrived(part, *evens(DIAG))
         relay(part, 1).start()
-
-    def far(part):
-        hand_all(part, FAR)
+        for chip in DIAG:
+            hand(part, chip).start()
 
     def send_late():
+        for chip in NEAR:
+            own(LATE, (*chip, 0)).start()
         own(LATE, SIB).start()
-        for chip in NEAR + DIAG:
-            own(LATE, (*chip, 0)).start()
-
+
+    acc[...] = jnp.zeros((STREAM, 128), F32)
     arrived(CH, SLOT[SIB])
-    one_pass(0, {0: lambda: hand_all(PK, NEAR)})
-    hand_all(PK, DIAG)
-    near(CH)
+    one_pass(0, {2: [lambda: near(CH), send_late, lambda: hand_all(PK, NEAR + DIAG)]})
     hand_all(PK, FAR)
+    arrived(CH, *odds(NEAR))
     arrived(PK, *range(1, OWNERS, 2))
-    send_late()
     ch[PICK_AT:PICK_AT + PICKS] = dot(pick_pack, pk[...].reshape(OWNERS * PCAP, width)).astype(BF16)
-    arrived(CH, *odds(NEAR))
-    acc[:PICK_AT] = jnp.zeros((PICK_AT, 128), F32)
-    one_pass(1, {0: lambda: diagonal(CH), 1: lambda: far(CH), 2: lambda: near(LATE)})
+    one_pass(1, {
+        0: [lambda: diagonal(CH)],
+        1: [lambda: near(LATE), lambda: hand_all(CH, FAR[:1])],
+        3: [lambda: hand_all(CH, FAR[1:]), lambda: diagonal(LATE)],
+    })
     cover_out.start()
-    arrived(CH, *odds(DIAG))
-    one_pass(2, {0: lambda: diagonal(LATE)})
-    far(LATE)
-    arrived(CH, *odds(FAR))
+    arrived(CH, *odds(DIAG + FAR[:1]))
+    one_pass(2, {
+        0: [lambda: hand_all(LATE, FAR[:1])],
+        2: [lambda: hand_all(LATE, FAR[1:])],
+    })
+    arrived(CH, *odds(FAR[1:]))
     arrived(LATE, *range(1, OWNERS, 2))
     packed = dot(ones_where(iota((REST, late_slots), 0).astype(F32) == late_row), late[...].reshape(late_slots, width))
     ch[REST_AT:] = packed.astype(BF16)
@@ -340,12 +359,11 @@
         share(rel, me).wait_send()
     for part in (PK, CH, LATE):
         own(part, SIB).wait_send()
-        for chip in NEAR + DIAG:
-            own(part, (*chip, 0)).wait_send()
-            hand(part, chip).wait_send()
-        for chip in FAR:
-            if part is PK:
+        for chip in NEAR + DIAG + FAR:
+            if part is PK or chip in NEAR:
                 own(part, (*chip, 0)).wait_send()
+            elif chip in DIAG:
+                across(part, chip[1]).wait_send()
             else:
                 relay(part, chip[0]).wait_send()
             hand(part, chip).wait_send()
@@ -383,7 +401,7 @@
 def per_device(embeddings, pick_index, cand_index):
     rows, width = embeddings.shape
     shift = rows.bit_length() - 1
-    chunks = 8
+    chunks = 4
     anywhere = pl.BlockSpec(memory_space=pl.ANY)
     dma = pltpu.SemaphoreType.DMA
     gains, cover, flag = pl.pallas_call(
@@ -402,7 +420,7 @@
             pltpu.VMEM((STREAM, width), BF16),
             pltpu.VMEM((OWNERS, UNIT, width), BF16),
             pltpu.VMEM((OWNERS, PCAP, width), BF16),
-            pltpu.VMEM((2 * UNIT, rows), F32),
+            pltpu.VMEM((PICK_AT, rows), F32),
             pltpu.VMEM((rows // 128, 128), F32),
             pltpu.VMEM((STREAM, 128), F32),
             pltpu.VMEM((OWNERS, 8, 128), F32),

time: 52.7 us -> 45 us (0.85)
  Pallas kernels: 49.1 us -> 41.4 us
    pallas_call x1, Pallas kernels: 49.1 us -> 41.4 us  [per_device(): pl.pallas_call(functools.partial(kernel, shift), out_shape=[jax.ShapeDtyp...]
where the time goes in v4:
time: 45 us; the launch traced here: 44.8 us
  Pallas kernels  41.4 us (92%)
  local copies, waits for them, and re-layouts  1.97 us (4%)
  between operations  1.22 us (3%)
    pallas_call x1, Pallas kernels, per_device(): pl.pallas_call(functools.partial(kernel, shift), out_shape=[jax.ShapeDtyp...  41.4 us
    unnamed x4, local copies, waits for them, and re-layouts  1.97 us

profile of v4, /device:TPU:1, one launch (start us, length us, event | category | flops | bytes accessed | tf_op | source)
XLA Modules:
  0.0 44.8 jit_solution(16690307666558856056)
XLA Ops:
  0.6 0.0 copy-start
  0.6 41.4 %shard_map.52 = (f32[8,128]{1,0:T(8,128)S(1)}, f32[64,128]{1,0:T(8,128)}, s32[1,1]{1,0:T(1,128)}) custom-call(s32[64,128]{1,0:T(8,128)} %bitcast.8, s32[1,64]{1,0:T(1,128)} %bitcast.9, bf16[8192,768]{1,0:T(8,128)(2,1)} %emb_hbm.1), custom_call_target="tpu_custom_call" | custom-call | flops 13690208256 | bytes 12582912 | tf_op jit(solution)/shard_map/pallas_call | solution.py:407
  42.6 0.0 copy-done
  42.6 0.2 conditional.1
  42.9 0.6 %copy.13 = f32[1024]{0:T(1024)} copy(f32[1024]{0:T(1024)S(1)} %get-tuple-element.35) | data formatting | bytes 8192
  43.5 1.4 %copy.14 = f32[8192]{0:T(1024)} copy(f32[8192]{0:T(1024)} %get-tuple-element.36) | data formatting | bytes 65536
Async XLA Ops:
  0.6 42.0 %copy-start = (s32[64]{0:T(128)S(1)}, s32[64]{0:T(128)}, u32[]{:S(2)}) copy-start(s32[64]{0:T(128)} %param.6) | copy-start | bytes 772

commit v5 on v4

--- a/solution.py
+++ b/solution.py
@@ -23,8 +23,7 @@
 PICK_AT = 2 * UNIT
 REST_AT = OWNERS * UNIT + PICKS
 STREAM = REST_AT + REST
-PASSES = ((0, PICK_AT), (PICK_AT, 448), (448, 736), (736, STREAM))
-STEP_ROWS = 2048
+PASSES = ((0, PICK_AT, 2048), (PICK_AT, 448, 2048), (448, 736, 2048), (736, STREAM, 8192))
 
 
 def unit_at(j):
@@ -61,7 +60,7 @@
     shift,
     cand_hbm, pick_hbm, emb_hbm,
     gains_ref, cover_hbm, flag_ref,
-    cand_ref, pick_ref, emb, ch, late, pk, raw, cover_ref, acc, red,
+    cand_ref, pick_ref, emb, ch, late, pk, pack, raw, cover_ref, acc, red,
     in_sem, load_sem, pk_send, pk_recv, ch_send, ch_recv, late_send, late_recv, red_send, red_recv,
 ):
     rows = emb.shape[0]
@@ -253,12 +252,12 @@
             acc[top:end] = part
 
     def one_pass(t, polls):
-        lo, hi = PASSES[t]
-        groups = STEP_ROWS // 128
+        lo, hi, step_rows = PASSES[t]
+        groups = step_rows // 128
 
         def step(i, carry):
-            at = pl.multiple_of(i * STEP_ROWS, STEP_ROWS)
-            s = inner(ch[lo:hi], emb[pl.ds(at, STEP_ROWS), :])
+            at = pl.multiple_of(i * step_rows, step_rows)
+            s = inner(ch[lo:hi], emb[pl.ds(at, step_rows), :])
 
             def kept(top, end, k):
                 return raw[top:end, pl.ds(pl.multiple_of(at + 128 * k, 128), 128)]
@@ -267,7 +266,7 @@
                 return s[top - lo:end - lo, 128 * k:128 * k + 128]
 
             if t == 0:
-                raw[:, pl.ds(at, STEP_ROWS)] = s
+                raw[:, pl.ds(at, step_rows)] = s
             elif t == 1:
                 cover = jnp.max(s[:PICKS], axis=0, keepdims=True)
                 covers = [cover[:, 128 * k:128 * k + 128] for k in range(groups)]
@@ -285,7 +284,15 @@
                         act()
             return carry
 
-        lax.fori_loop(0, rows // STEP_ROWS, step, 0)
+        lax.fori_loop(0, rows // step_rows, step, 0)
+
+    def in_place(lo, hi):
+        found = jnp.sum(acc[lo:hi], axis=1, keepdims=True)
+        row = (iota((hi - lo, 128), 0) + lo).astype(F32)
+        parts = [
+            jnp.sum(jnp.where(row == place[r:r + 1], found, 0.0), axis=0, keepdims=True) for r in range(8)
+        ]
+        return jnp.concatenate(parts, axis=0)
 
     def hand_all(part, chips):
         arrived(part, *evens(chips))
@@ -312,6 +319,7 @@
         own(LATE, SIB).start()
 
     acc[...] = jnp.zeros((STREAM, 128), F32)
+    pack[...] = ones_where(iota((REST, late_slots), 0).astype(F32) == late_row)
     arrived(CH, SLOT[SIB])
     one_pass(0, {2: [lambda: near(CH), send_late, lambda: hand_all(PK, NEAR + DIAG)]})
     hand_all(PK, FAR)
@@ -329,18 +337,14 @@
         0: [lambda: hand_all(LATE, FAR[:1])],
         2: [lambda: hand_all(LATE, FAR[1:])],
     })
+    red[me] = in_place(0, PASSES[3][0])
     arrived(CH, *odds(FAR[1:]))
     arrived(LATE, *range(1, OWNERS, 2))
-    packed = dot(ones_where(iota((REST, late_slots), 0).astype(F32) == late_row), late[...].reshape(late_slots, width))
+    packed = dot(pack[...], late[...].reshape(late_slots, width))
     ch[REST_AT:] = packed.astype(BF16)
     one_pass(3, {})
 
-    found = jnp.sum(acc[...], axis=1, keepdims=True)
-    dense_at = iota((STREAM, 128), 0).astype(F32)
-    parts = []
-    for r in range(8):
-        parts.append(jnp.sum(jnp.where(dense_at == place[r:r + 1], found, 0.0), axis=0, keepdims=True))
-    red[me] = jnp.concatenate(parts, axis=0)
+    red[me] += in_place(PASSES[3][0], STREAM)
 
     def share(rel, at):
         return remote(red.at[me], red.at[at], red_send.at[SLOT[rel]], red_recv.at[at], device(*rel))
@@ -396,6 +400,17 @@
     similar = inner(embeddings, chosen)
     partial = jnp.sum(jnp.maximum(similar - coverage[:, None], 0.0), axis=0)
     return sum_over_rows(partial) / (count * lax.axis_size("row")), coverage
+
+
+def settle(gains, cover, gains_out, cover_out, sem):
+    copies = [
+        pltpu.make_async_copy(gains, gains_out, sem.at[0]),
+        pltpu.make_async_copy(cover, cover_out, sem.at[1]),
+    ]
+    for copy in copies:
+        copy.start()
+    for copy in copies:
+        copy.wait()
 
 
 def per_device(embeddings, pick_index, cand_index):
@@ -420,6 +435,7 @@
             pltpu.VMEM((STREAM, width), BF16),
             pltpu.VMEM((OWNERS, UNIT, width), BF16),
             pltpu.VMEM((OWNERS, PCAP, width), BF16),
+            pltpu.VMEM((REST, OWNERS * UNIT), BF16),
             pltpu.VMEM((PICK_AT, rows), F32),
             pltpu.VMEM((rows // 128, 128), F32),
             pltpu.VMEM((STREAM, 128), F32),
@@ -431,11 +447,18 @@
         cost_estimate=pl.CostEstimate(
             flops=2 * rows * (PER + PICKS) * width, bytes_accessed=2 * rows * width, transcendentals=0),
     )(cand_index.reshape(-1, 128), pick_index.reshape(1, PICKS), embeddings)
+
+    def fast_path():
+        in_hbm = pl.BlockSpec(memory_space=pltpu.HBM)
+        outs = pl.pallas_call(
+            settle,
+            out_shape=[jax.ShapeDtypeStruct(x.shape, F32) for x in (gains, cover)],
+            in_specs=[anywhere] * 2, out_specs=[in_hbm] * 2, scratch_shapes=[dma((2,))],
+        )(gains, cover)
+        return outs[0].reshape(PER), outs[1].reshape(rows)
+
     return lax.cond(
-        flag[0, 0] == 0,
-        lambda: (gains.reshape(PER), cover.reshape(rows)),
-        lambda: whole_path(embeddings, pick_index, cand_index),
-    )
+        flag[0, 0] == 0, fast_path, lambda: whole_path(embeddings, pick_index, cand_index))
 
 
 def solution(mesh):

time: 45 us -> 43.6 us (0.969)
  local copies, waits for them, and re-layouts: 1.97 us -> 0.59 us
    unnamed x4, local copies, waits for them, and re-layouts: 1.97 us -> 0.59 us
    pallas_call x1, Pallas kernels: 41.4 us -> 40.7 us  [per_device(): pl.pallas_call(functools.partial(kernel, shift), out_shape=[jax.ShapeDtyp...]
    pallas_call x0 -> x1, Pallas kernels: none -> 0.64 us  [fast_path(): pl.pallas_call(settle, out_shape=[jax.ShapeDtypeStruct(x.shape, F32) for...]
where the time goes in v5:
time: 43.6 us; the launch traced here: 43.4 us
  Pallas kernels  41.3 us (95%)
  between operations  1.31 us (3%)
  local copies, waits for them, and re-layouts  0.59 us (1%)
    pallas_call x1, Pallas kernels, per_device(): pl.pallas_call(functools.partial(kernel, shift), out_shape=[jax.ShapeDtyp...  40.7 us

profile of v5, /device:TPU:1, one launch (start us, length us, event | category | flops | bytes accessed | tf_op | source)
XLA Modules:
  0.0 43.4 jit_solution(1661119313212466644)
XLA Ops:
  0.6 0.0 copy-start.2
  0.6 40.7 %shard_map.52 = (f32[8,128]{1,0:T(8,128)S(1)}, f32[64,128]{1,0:T(8,128)S(1)}, s32[1,1]{1,0:T(1,128)}) custom-call(s32[64,128]{1,0:T(8,128)} %bitcast.9, s32[1,64]{1,0:T(1,128)} %bitcast.10, bf16[8192,768]{1,0:T(8,128)(2,1)} %emb_hbm.1), custom_call_target="tpu_custom_call" | custom-call | flops 13690208256 | bytes 12582912 | tf_op jit(solution)/shard_map/pallas_call | solution.py:422
  41.9 0.0 copy-done.2
  42.0 0.9 %conditional.1 = (f32[8192]{0:T(1024)}, f32[1024]{0:T(1024)S(1)}) conditional(s32[]{:T(128)} %bitcast.4, (s32[8192]{0:T(1024)}, bf16[8192,768]{1,0:T(8,128)(2,1)}, s32[64]{0:T(128)S(1)}) %tuple.24, (f32[8,128]{1,0:T(8,128)S(1)}, f32[64,128]{1,0:T(8,128)S(1)}) %tuple.16), branch_computations={%region_0.3_spmd, %region_3.4_spmd} | conditional | flops 13722598400 | bytes 77316112 | solution.py:460
  42.2 0.6 %branch_1_fun.1 = (f32[8,128]{1,0:T(8,128)S(1)}, f32[64,128]{1,0:T(8,128)}) custom-call(f32[8,128]{1,0:T(8,128)S(1)} %get-tuple-element.13.gains, f32[64,128]{1,0:T(8,128)S(1)} %get-tuple-element.14.cover), custom_call_target="tpu_custom_call" | custom-call | tf_op jit(solution)/shard_map/cond/branch_1_fun/pallas_call | solution.py:453
  42.8 0.0 copy-start.1
  42.9 0.6 %copy-done.1 = f32[1024]{0:T(1024)} copy-done((f32[1024]{0:T(1024)}, f32[1024]{0:T(1024)S(1)}, u32[]{:S(2)}) %copy-start.1) | copy-done | bytes 4120
Async XLA Ops:
  0.6 41.3 %copy-start.2 = (s32[64]{0:T(128)S(1)}, s32[64]{0:T(128)}, u32[]{:S(2)}) copy-start(s32[64]{0:T(128)} %param.6) | copy-start | bytes 772
  42.8 0.6 %copy-start.1 = (f32[1024]{0:T(1024)}, f32[1024]{0:T(1024)S(1)}, u32[]{:S(2)}) copy-start(f32[1024]{0:T(1024)S(1)} %get-tuple-element.25) | copy-start | bytes 12292

commit v6 on v5

--- a/solution.py
+++ b/solution.py
@@ -23,7 +23,7 @@
 PICK_AT = 2 * UNIT
 REST_AT = OWNERS * UNIT + PICKS
 STREAM = REST_AT + REST
-PASSES = ((0, PICK_AT, 2048), (PICK_AT, 448, 2048), (448, 736, 2048), (736, STREAM, 8192))
+PASSES = ((0, PICK_AT, 2048), (PICK_AT, 448, 4096), (448, 736, 4096), (736, STREAM, 8192))
 
 
 def unit_at(j):
@@ -83,7 +83,7 @@
     cover_out = pltpu.make_async_copy(cover_ref, cover_hbm, in_sem.at[2])
     cand_in.start()
     pick_in.start()
-    for i in range(chunks):
+    for i in range(2):
         load(i).start()
 
     barrier = pltpu.get_barrier_semaphore()
@@ -125,6 +125,11 @@
 
     def gather(i, total):
         load(i).wait()
+
+        @pl.when(i + 2 < chunks)
+        def _():
+            load(i + 2).start()
+
         at = pl.ds(pl.multiple_of(i * chunk, chunk), chunk)
         return total + dot(ones_where(at_row - i * chunk == lanes), emb[at, :])
 
@@ -185,6 +190,7 @@
         for j in js:
             remote(block(0), block(j), sent.at[j], got.at[j], device(0, 0, 1)).wait_recv()
 
+    STRAIGHT = (PK, LATE)
     SIB = (0, 0, 1)
     NEAR = ((1, 0), (0, 1), (0, 3))
     DIAG = ((1, 1), (1, 3))
@@ -199,6 +205,8 @@
     for chip in NEAR:
         own(CH, (*chip, 0)).start()
     own(CH, SIB).start()
+    if CH in STRAIGHT:
+        own(CH, (*FAR[1], 0)).start()
     for chip in FAR + DIAG + NEAR:
         own(PK, (*chip, 0)).start()
     own(PK, SIB).start()
@@ -309,7 +317,8 @@
 
     def diagonal(part):
         arrived(part, *evens(DIAG))
-        relay(part, 1).start()
+        if part not in STRAIGHT:
+            relay(part, 1).start()
         for chip in DIAG:
             hand(part, chip).start()
 
@@ -317,6 +326,8 @@
         for chip in NEAR:
             own(LATE, (*chip, 0)).start()
         own(LATE, SIB).start()
+        if LATE in STRAIGHT:
+            own(LATE, (*FAR[1], 0)).start()
 
     acc[...] = jnp.zeros((STREAM, 128), F32)
     pack[...] = ones_where(iota((REST, late_slots), 0).astype(F32) == late_row)
@@ -327,16 +338,12 @@
     arrived(PK, *range(1, OWNERS, 2))
     ch[PICK_AT:PICK_AT + PICKS] = dot(pick_pack, pk[...].reshape(OWNERS * PCAP, width)).astype(BF16)
     one_pass(1, {
-        0: [lambda: diagonal(CH)],
-        1: [lambda: near(LATE), lambda: hand_all(CH, FAR[:1])],
-        3: [lambda: hand_all(CH, FAR[1:]), lambda: diagonal(LATE)],
+        0: [lambda: diagonal(CH), lambda: hand_all(CH, FAR[:1]), lambda: near(LATE)],
+        1: [lambda: hand_all(CH, FAR[1:]), lambda: hand_all(LATE, FAR[1:])],
     })
     cover_out.start()
     arrived(CH, *odds(DIAG + FAR[:1]))
-    one_pass(2, {
-        0: [lambda: hand_all(LATE, FAR[:1])],
-        2: [lambda: hand_all(LATE, FAR[1:])],
-    })
+    one_pass(2, {0: [lambda: diagonal(LATE), lambda: hand_all(LATE, FAR[:1])]})
     red[me] = in_place(0, PASSES[3][0])
     arrived(CH, *odds(FAR[1:]))
     arrived(LATE, *range(1, OWNERS, 2))
@@ -364,7 +371,7 @@
     for part in (PK, CH, LATE):
         own(part, SIB).wait_send()
         for chip in NEAR + DIAG + FAR:
-            if part is PK or chip in NEAR:
+            if part is PK or chip in NEAR or (chip == FAR[1] and part in STRAIGHT):
                 own(part, (*chip, 0)).wait_send()
             elif chip in DIAG:
                 across(part, chip[1]).wait_send()

time: 43.6 us -> 42 us (0.963)
  Pallas kernels: 41.3 us -> 39.7 us
    pallas_call x1, Pallas kernels: 40.7 us -> 39 us  [per_device(): pl.pallas_call(functools.partial(kernel, shift), out_shape=[jax.ShapeDtyp...]
where the time goes in v6:
time: 42 us; the launch traced here: 41.8 us
  Pallas kernels  39.7 us (95%)
  between operations  1.31 us (3%)
  local copies, waits for them, and re-layouts  0.59 us (1%)
    pallas_call x1, Pallas kernels, per_device(): pl.pallas_call(functools.partial(kernel, shift), out_shape=[jax.ShapeDtyp...  39 us

profile of v6, /device:TPU:1, one launch (start us, length us, event | category | flops | bytes accessed | tf_op | source)
XLA Modules:
  0.0 41.8 jit_solution(376940849346218643)
XLA Ops:
  0.6 0.0 copy-start.2
  0.6 39.0 %shard_map.52 = (f32[8,128]{1,0:T(8,128)S(1)}, f32[64,128]{1,0:T(8,128)S(1)}, s32[1,1]{1,0:T(1,128)}) custom-call(s32[64,128]{1,0:T(8,128)} %bitcast.9, s32[1,64]{1,0:T(1,128)} %bitcast.10, bf16[8192,768]{1,0:T(8,128)(2,1)} %emb_hbm.1), custom_call_target="tpu_custom_call" | custom-call | flops 13690208256 | bytes 12582912 | tf_op jit(solution)/shard_map/pallas_call | solution.py:429
  40.3 0.0 copy-done.2
  40.3 0.9 %conditional.1 = (f32[8192]{0:T(1024)}, f32[1024]{0:T(1024)S(1)}) conditional(s32[]{:T(128)} %bitcast.4, (s32[8192]{0:T(1024)}, bf16[8192,768]{1,0:T(8,128)(2,1)}, s32[64]{0:T(128)S(1)}) %tuple.24, (f32[8,128]{1,0:T(8,128)S(1)}, f32[64,128]{1,0:T(8,128)S(1)}) %tuple.16), branch_computations={%region_0.3_spmd, %region_3.4_spmd} | conditional | flops 13722598400 | bytes 77316112 | solution.py:467
  40.6 0.6 %branch_1_fun.1 = (f32[8,128]{1,0:T(8,128)S(1)}, f32[64,128]{1,0:T(8,128)}) custom-call(f32[8,128]{1,0:T(8,128)S(1)} %get-tuple-element.13.gains, f32[64,128]{1,0:T(8,128)S(1)} %get-tuple-element.14.cover), custom_call_target="tpu_custom_call" | custom-call | tf_op jit(solution)/shard_map/cond/branch_1_fun/pallas_call | solution.py:460
  41.2 0.0 copy-start.1
  41.2 0.6 %copy-done.1 = f32[1024]{0:T(1024)} copy-done((f32[1024]{0:T(1024)}, f32[1024]{0:T(1024)S(1)}, u32[]{:S(2)}) %copy-start.1) | copy-done | bytes 4120
Async XLA Ops:
  0.6 39.7 %copy-start.2 = (s32[64]{0:T(128)S(1)}, s32[64]{0:T(128)}, u32[]{:S(2)}) copy-start(s32[64]{0:T(128)} %param.6) | copy-start | bytes 772
  41.2 0.6 %copy-start.1 = (f32[1024]{0:T(1024)}, f32[1024]{0:T(1024)S(1)}, u32[]{:S(2)}) copy-start(f32[1024]{0:T(1024)S(1)} %get-tuple-element.25) | copy-start | bytes 12292

commit v7 on v6

--- a/solution.py
+++ b/solution.py
@@ -332,7 +332,7 @@
     acc[...] = jnp.zeros((STREAM, 128), F32)
     pack[...] = ones_where(iota((REST, late_slots), 0).astype(F32) == late_row)
     arrived(CH, SLOT[SIB])
-    one_pass(0, {2: [lambda: near(CH), send_late, lambda: hand_all(PK, NEAR + DIAG)]})
+    one_pass(0, {2: [lambda: near(CH), send_late], 3: [lambda: hand_all(PK, NEAR + DIAG)]})
     hand_all(PK, FAR)
     arrived(CH, *odds(NEAR))
     arrived(PK, *range(1, OWNERS, 2))

time: 42 us -> 42 us (level)
  no operation moved by 1% of the time
where the time goes in v7:
time: 42 us; the launch traced here: 41.9 us
  Pallas kernels  39.7 us (95%)
  between operations  1.31 us (3%)
  local copies, waits for them, and re-layouts  0.59 us (1%)
    pallas_call x1, Pallas kernels, per_device(): pl.pallas_call(functools.partial(kernel, shift), out_shape=[jax.ShapeDtyp...  39.1 us

profile of v7, /device:TPU:1, one launch (start us, length us, event | category | flops | bytes accessed | tf_op | source)
XLA Modules:
  0.0 41.9 jit_solution(13941346658394325827)
XLA Ops:
  0.6 0.0 copy-start.2
  0.6 39.1 %shard_map.52 = (f32[8,128]{1,0:T(8,128)S(1)}, f32[64,128]{1,0:T(8,128)S(1)}, s32[1,1]{1,0:T(1,128)}) custom-call(s32[64,128]{1,0:T(8,128)} %bitcast.9, s32[1,64]{1,0:T(1,128)} %bitcast.10, bf16[8192,768]{1,0:T(8,128)(2,1)} %emb_hbm.1), custom_call_target="tpu_custom_call" | custom-call | flops 13690208256 | bytes 12582912 | tf_op jit(solution)/shard_map/pallas_call | solution.py:429
  40.4 0.0 copy-done.2
  40.4 0.9 %conditional.1 = (f32[8192]{0:T(1024)}, f32[1024]{0:T(1024)S(1)}) conditional(s32[]{:T(128)} %bitcast.4, (s32[8192]{0:T(1024)}, bf16[8192,768]{1,0:T(8,128)(2,1)}, s32[64]{0:T(128)S(1)}) %tuple.24, (f32[8,128]{1,0:T(8,128)S(1)}, f32[64,128]{1,0:T(8,128)S(1)}) %tuple.16), branch_computations={%region_0.3_spmd, %region_3.4_spmd} | conditional | flops 13722598400 | bytes 77316112 | solution.py:467
  40.6 0.6 %branch_1_fun.1 = (f32[8,128]{1,0:T(8,128)S(1)}, f32[64,128]{1,0:T(8,128)}) custom-call(f32[8,128]{1,0:T(8,128)S(1)} %get-tuple-element.13.gains, f32[64,128]{1,0:T(8,128)S(1)} %get-tuple-element.14.cover), custom_call_target="tpu_custom_call" | custom-call | tf_op jit(solution)/shard_map/cond/branch_1_fun/pallas_call | solution.py:460
  41.3 0.0 copy-start.1
  41.3 0.6 %copy-done.1 = f32[1024]{0:T(1024)} copy-done((f32[1024]{0:T(1024)}, f32[1024]{0:T(1024)S(1)}, u32[]{:S(2)}) %copy-start.1) | copy-done | bytes 4120
Async XLA Ops:
  0.6 39.8 %copy-start.2 = (s32[64]{0:T(128)S(1)}, s32[64]{0:T(128)}, u32[]{:S(2)}) copy-start(s32[64]{0:T(128)} %param.6) | copy-start | bytes 772
  41.3 0.6 %copy-start.1 = (f32[1024]{0:T(1024)}, f32[1024]{0:T(1024)S(1)}, u32[]{:S(2)}) copy-start(f32[1024]{0:T(1024)S(1)} %get-tuple-element.25) | copy-start | bytes 12292
